TPU v7x, 512 devices: a whole 4x8x8 slice. The times are simulated.
512 devices in a mesh: shell: 64 (over x, y, z_lo), lat: 8 (over z_hi, core).
Axes of the slice: x: 4, y: 8, z: 8 (z_hi: 4, z_lo: 2; z = z_hi * 2 + z_lo), core: 2. Of those that a mesh axis runs over, the one named last changes fastest.
Arguments:
- advective_warming: bfloat16 [256, 768, 1536], P('shell', 'lat'), may hold values from -6 to 6
- associated_polynomial_table: bfloat16 [128, 768, 512], P(None, 'lat', 'shell'), may hold values from -12 to 12, as said below
- thermal_field: float32 [512, 128, 2, 256], P('shell', 'lat'), may hold values from -6 to 6
- operator_reciprocal: float32 [512, 256, 256], P('shell'), may hold values from -1 to 3, as said below
Outputs:
- new_temperature: float32 [512, 128, 2, 256], P('shell', 'lat')
Inputs may be any that keep to these rules, and one draw needn't show every extreme that they name: `associated_polynomial_table`: zero wherever the degree l is below the order j * 4. `operator_reciprocal`: one matrix of order 256 for each degree.
All inputs are finite; a program needn't handle non-finite values.
Results may differ from a plain program's by a relative error of at most 0.007.
Values may be sent and summed in bfloat16 or wider, within the bound.
A program may use at most 128 MiB of HBM per device.

v0:
```python
import math
import jax
import jax.numpy as jnp
import numpy as np
from jax import lax
from jax.sharding import Mesh, PartitionSpec as P

backward_euler_update = 0.5


def analysis_rows(orders, stride, longitudes):
    phase = np.arange(orders)[:, None] * stride * np.arange(longitudes)[None, :] % longitudes
    angles = phase.astype(np.float32) * np.float32(2.0 * math.pi / longitudes)
    stacked = np.stack([np.cos(angles), -np.sin(angles)], axis=1) / np.float32(longitudes)
    return jnp.asarray(stacked.reshape(2 * orders, longitudes)).astype(jnp.bfloat16)


def shards(advective_warming, table, thermal_field, operator_reciprocal):
    radial_levels, bands, longitudes = advective_warming.shape
    orders = table.shape[0]
    own_degrees = table.shape[2]
    degrees = own_degrees * lax.axis_size("x") * lax.axis_size("g")
    table = lax.all_to_all(table, "lat", split_axis=0, concat_axis=1, tiled=True)
    table = lax.all_to_all(table, "g", split_axis=0, concat_axis=2, tiled=True)
    table = lax.all_gather(table, "x", axis=2, tiled=True)
    analysis = analysis_rows(orders, degrees // orders, longitudes)
    fourier = lax.dot_general(
        analysis,
        advective_warming.reshape(radial_levels * bands, longitudes),
        (((1,), (1,)), ((), ())),
        preferred_element_type=jnp.float32,
    )
    fourier = fourier.astype(jnp.bfloat16).reshape(orders, 2, radial_levels, bands)
    fourier = lax.all_to_all(fourier, "lat", split_axis=0, concat_axis=3, tiled=True)
    fourier = lax.all_to_all(fourier, "g", split_axis=0, concat_axis=2, tiled=True)
    block = jnp.einsum("mcrt,mtl->mcrl", fourier, table, preferred_element_type=jnp.float32)
    own_levels = block.shape[2]
    block = lax.all_to_all(
        block.astype(jnp.bfloat16), ("x", "g"), split_axis=3, concat_axis=0, tiled=True
    ).astype(jnp.float32)
    block = block.reshape(-1, thermal_field.shape[1], 2, own_levels, own_degrees)
    block = jnp.transpose(block, (4, 1, 2, 0, 3)).reshape(thermal_field.shape)
    forcing = thermal_field + backward_euler_update * block
    return jnp.einsum(
        "lij,lmcj->lmci", operator_reciprocal, forcing, precision=lax.Precision.HIGHEST
    )


def solution(mesh):
    shells, lats = mesh.devices.shape
    finer = Mesh(mesh.devices.reshape(4, shells // 4, lats), ("x", "g", "lat"))
    shell = ("x", "g")
    in_specs = (
        P(shell, "lat", None),
        P(None, "lat", shell),
        P(shell, "lat", None, None),
        P(shell, None, None),
    )
    out_specs = P(shell, "lat", None, None)
    return jax.shard_map(
        shards, mesh=finer, in_specs=in_specs, out_specs=out_specs, check_vma=False
    )
```

profile of v0, /device:TPU:8, one launch (start us, length us, event | category | flops | bytes accessed | tf_op | source)
XLA Modules:
  0.0 108.8 jit_solution(15241552492936182516)
XLA Ops:
  0.0 0.0 copy-start
  0.0 2.2 %convolution_convert_fusion = bf16[256,384]{1,0:T(8,128)(2,1)S(1)} fusion(bf16[256,1536]{1,0:T(8,128)(2,1)} %constant.9, bf16[384,1536]{1,0:T(8,128)(2,1)} %bitcast.51), kind=kOutput, calls=%fused_computation.2 | convolution fusion | flops 302088192 | bytes 2162688 | tf_op jit(solution)/shard_map/dot_general | solution.py:27
  2.3 0.9 reshape.26
  3.1 10.3 %all-to-all-start = ((bf16[128,2,4,96]{3,2,1,0:T(4,128)(2,1)}), bf16[128,2,4,96]{3,2,1,0:T(4,128)(2,1)S(1)}, u32[]{:S(2)}, u32[]{:S(2)}) async-start(bf16[128,2,4,96]{3,2,1,0:T(4,128)(2,1)} %reshape.26), calls=%async_computation | async-start | bytes 524288 | tf_op jit(solution)/shard_map/all_to_all | solution.py:34
  13.4 0.0 copy-done.2
  13.5 0.9 copy.28
  14.4 11.8 %all-to-all-done = bf16[128,2,4,96]{3,2,1,0:T(4,128)(2,1)S(1)} async-done(((bf16[128,2,4,96]{3,2,1,0:T(4,128)(2,1)}), bf16[128,2,4,96]{3,2,1,0:T(4,128)(2,1)S(1)}, u32[]{:S(2)}, u32[]{:S(2)}) %all-to-all-start) | async-done | bytes 196640 | tf_op jit(solution)/shard_map/all_to_all | solution.py:34
  26.2 3.4 %all-to-all-start.2 = ((bf16[128,96,8]{1,2,0:T(8,128)(2,1)}), bf16[128,96,8]{1,2,0:T(8,128)(2,1)S(1)}, u32[]{:S(2)}, u32[]{:S(2)}) async-start(bf16[128,96,8]{1,2,0:T(8,128)(2,1)} %copy.28), calls=%async_computation.2 | async-start | bytes 524288 | tf_op jit(solution)/shard_map/all_to_all | solution.py:23
  29.6 0.3 copy.26
  29.9 0.9 all_to_all.60
  30.9 10.8 %all-to-all-done.2 = bf16[128,96,8]{1,2,0:T(8,128)(2,1)S(1)} async-done(((bf16[128,96,8]{1,2,0:T(8,128)(2,1)}), bf16[128,96,8]{1,2,0:T(8,128)(2,1)S(1)}, u32[]{:S(2)}, u32[]{:S(2)}) %all-to-all-start.2) | async-done | bytes 196640 | tf_op jit(solution)/shard_map/all_to_all | solution.py:23
  41.6 8.3 %all-to-all-start.1 = ((bf16[16,2,4,768]{3,2,1,0:T(4,128)(2,1)}), bf16[16,2,4,768]{3,2,1,0:T(4,128)(2,1)S(1)}, u32[]{:S(2)}, u32[]{:S(2)}) async-start(bf16[16,2,4,768]{3,2,1,0:T(4,128)(2,1)} %all_to_all.60), calls=%async_computation.1 | async-start | bytes 393216 | tf_op jit(solution)/shard_map/all_to_all | solution.py:35
  49.9 0.2 copy.29
  50.1 0.9 all_to_all.67
  51.0 7.7 %all-to-all-done.1 = bf16[16,2,4,768]{3,2,1,0:T(4,128)(2,1)S(1)} async-done(((bf16[16,2,4,768]{3,2,1,0:T(4,128)(2,1)}), bf16[16,2,4,768]{3,2,1,0:T(4,128)(2,1)S(1)}, u32[]{:S(2)}, u32[]{:S(2)}) %all-to-all-start.1) | async-done | bytes 196640 | tf_op jit(solution)/shard_map/all_to_all | solution.py:35
  58.8 4.8 %all-to-all-start.3 = ((bf16[16,768,8]{1,2,0:T(8,128)(2,1)}), bf16[16,768,8]{1,2,0:T(8,128)(2,1)S(1)}, u32[]{:S(2)}, u32[]{:S(2)}) async-start(bf16[16,768,8]{1,2,0:T(8,128)(2,1)} %all_to_all.67), calls=%async_computation.3 | async-start | bytes 393216 | tf_op jit(solution)/shard_map/all_to_all | solution.py:24
  63.6 0.1 copy.27
  63.6 0.1 reshape.27
  63.7 8.7 %all-to-all-done.3 = bf16[16,768,8]{1,2,0:T(8,128)(2,1)S(1)} async-done(((bf16[16,768,8]{1,2,0:T(8,128)(2,1)}), bf16[16,768,8]{1,2,0:T(8,128)(2,1)S(1)}, u32[]{:S(2)}, u32[]{:S(2)}) %all-to-all-start.3) | async-done | bytes 196640 | tf_op jit(solution)/shard_map/all_to_all | solution.py:24
  72.4 0.2 copy.30
  72.5 16.0 %all_gather.3 = bf16[1,768,512]{2,1,0:T(8,128)(2,1)S(1)} all-gather(bf16[1,768,128]{2,1,0:T(8,128)(2,1)S(1)} %copy.30), channel_id=1, replica_groups=mesh['x'=4,'g'=16,'lat'=8] {'x'}, dimensions={2}, use_global_device_ids=true | all-gather | bytes 983040 | tf_op jit(solution)/shard_map/all_gather | solution.py:25
  88.5 0.3 fusion.2
  88.8 0.0 copy-start.1
  88.8 0.2 copy.31
  88.9 0.2 reshape.34
  89.1 15.6 %all_to_all.78 = bf16[64,2,512]{2,1,0:T(2,128)(2,1)S(1)} all-to-all(bf16[64,2,512]{2,1,0:T(2,128)(2,1)S(1)} %reshape.34), channel_id=1, replica_groups=mesh['x'=4,'g'=16,'lat'=8] {'x','g'}, dimensions={0} | all-to-all | bytes 262144 | tf_op jit(solution)/shard_map/all_to_all | solution.py:38
  104.7 0.2 reshape.35
  105.0 0.3 copy.33
  105.3 0.4 mul.23
  105.7 0.1 add.3
  105.9 2.0 %fusion = f32[8,16,2,256]{3,1,2,0:T(8,128)S(1)} fusion(f32[8,256,256]{2,1,0:T(8,128)S(1)} %copy-done, f32[8,16,2,256]{3,2,1,0:T(2,128)S(1)} %add.3), kind=kOutput, calls=%fused_computation | convolution fusion | flops 201326592 | bytes 2621440 | tf_op jit(solution)/shard_map/lij,lmcj->lmci/dot_general | solution.py:44
  107.9 0.9 copy.35
  (4 shorter events, 0.0 us)
Async XLA Ops:
  0.0 105.9 %copy-start = (f32[8,256,256]{2,1,0:T(8,128)S(1)}, f32[8,256,256]{2,1,0:T(8,128)}, u32[]{:S(2)}) copy-start(f32[8,256,256]{2,1,0:T(8,128)} %param.8) | copy-start | bytes 6291460
  0.0 13.4 %copy-start.2 = (bf16[128,96,8]{0,2,1:T(8,128)(2,1)S(1)}, bf16[128,96,8]{0,2,1:T(8,128)(2,1)}, u32[]{:S(2)}) copy-start(bf16[128,96,8]{0,2,1:T(8,128)(2,1)} %param.6) | copy-start | bytes 589828
  3.1 23.1 %all-to-all-start = ((bf16[128,2,4,96]{3,2,1,0:T(4,128)(2,1)}), bf16[128,2,4,96]{3,2,1,0:T(4,128)(2,1)S(1)}, u32[]{:S(2)}, u32[]{:S(2)}) async-start(bf16[128,2,4,96]{3,2,1,0:T(4,128)(2,1)} %reshape.26), calls=%async_computation | async-start | bytes 524288 | tf_op jit(solution)/shard_map/all_to_all | solution.py:34
  26.2 15.4 %all-to-all-start.2 = ((bf16[128,96,8]{1,2,0:T(8,128)(2,1)}), bf16[128,96,8]{1,2,0:T(8,128)(2,1)S(1)}, u32[]{:S(2)}, u32[]{:S(2)}) async-start(bf16[128,96,8]{1,2,0:T(8,128)(2,1)} %copy.28), calls=%async_computation.2 | async-start | bytes 524288 | tf_op jit(solution)/shard_map/all_to_all | solution.py:23
  41.6 17.1 %all-to-all-start.1 = ((bf16[16,2,4,768]{3,2,1,0:T(4,128)(2,1)}), bf16[16,2,4,768]{3,2,1,0:T(4,128)(2,1)S(1)}, u32[]{:S(2)}, u32[]{:S(2)}) async-start(bf16[16,2,4,768]{3,2,1,0:T(4,128)(2,1)} %all_to_all.60), calls=%async_computation.1 | async-start | bytes 393216 | tf_op jit(solution)/shard_map/all_to_all | solution.py:35
  58.8 13.6 %all-to-all-start.3 = ((bf16[16,768,8]{1,2,0:T(8,128)(2,1)}), bf16[16,768,8]{1,2,0:T(8,128)(2,1)S(1)}, u32[]{:S(2)}, u32[]{:S(2)}) async-start(bf16[16,768,8]{1,2,0:T(8,128)(2,1)} %all_to_all.67), calls=%async_computation.3 | async-start | bytes 393216 | tf_op jit(solution)/shard_map/all_to_all | solution.py:24
  88.8 17.0 %copy-start.1 = (f32[8,16,2,256]{3,2,1,0:T(2,128)S(1)}, f32[8,16,2,256]{3,2,1,0:T(2,128)}, u32[]{:S(2)}) copy-start(f32[8,16,2,256]{3,2,1,0:T(2,128)} %param.7) | copy-start | bytes 786436
where the time goes:
time: 109 us
  waiting for transfers between devices  39 us (36%)
  blocking collectives  31.5 us (29%)
  starting transfers between devices  26.8 us (25%)
  local copies, waits for them, and re-layouts  6.65 us (6%)
  matrix products  4.53 us (4%)
    all_gather x1, blocking collectives, shards(): table = lax.all_gather(table, 'x', axis=2, tiled=True)  16 us
    all_to_all x1, blocking collectives, shards(): lax.all_to_all(block.astype(jnp.bfloat16), ('x', 'g'), split_axis=3, conc...  15.6 us
    all_to_all x1, waiting for transfers between devices, shards(): lax.all_to_all(fourier, 'lat', split_axis=0, concat_axis=3, tiled=True)  11.8 us
    all_to_all x1, waiting for transfers between devices, shards(): lax.all_to_all(table, 'lat', split_axis=0, concat_axis=1, tiled=True)  10.8 us
    all_to_all x1, starting transfers between devices, shards(): lax.all_to_all(fourier, 'lat', split_axis=0, concat_axis=3, tiled=True)  10.3 us
    all_to_all x1, waiting for transfers between devices, shards(): table = lax.all_to_all(table, 'g', split_axis=0, concat_axis=2, tiled=True)  8.67 us
    all_to_all x1, starting transfers between devices, shards(): lax.all_to_all(fourier, 'g', split_axis=0, concat_axis=2, tiled=True)  8.3 us
    all_to_all x1, waiting for transfers between devices, shards(): lax.all_to_all(fourier, 'g', split_axis=0, concat_axis=2, tiled=True)  7.73 us
  transfers between devices with their start and end apart: 4, of which 4 were waited for; matrix products, arithmetic and copies ran while one was open for 1% of the time, Pallas kernels for 0%

commit v1 on v0

--- a/solution.py
+++ b/solution.py
@@ -22,7 +22,9 @@
     degrees = own_degrees * lax.axis_size("x") * lax.axis_size("g")
     table = lax.all_to_all(table, "lat", split_axis=0, concat_axis=1, tiled=True)
     table = lax.all_to_all(table, "g", split_axis=0, concat_axis=2, tiled=True)
-    table = lax.all_gather(table, "x", axis=2, tiled=True)
+    table = jnp.concatenate(
+        lax.all_to_all(jnp.stack([table] * lax.axis_size("x")), "x", 0, 0), axis=2
+    )
     analysis = analysis_rows(orders, degrees // orders, longitudes)
     fourier = lax.dot_general(
         analysis,

time: 109 us -> 110 us (level)
  blocking collectives: 31.5 us -> 14.9 us
  waiting for transfers between devices: 39 us -> 46.3 us
  local copies, waits for them, and re-layouts: 6.65 us -> 11.9 us
  starting transfers between devices: 26.8 us -> 31.1 us
    all_gather x1 -> x0, blocking collectives: 16 us -> none  [shards(): table = lax.all_gather(table, 'x', axis=2, tiled=True)]
    all_to_all x0 -> x1, waiting for transfers between devices: none -> 9.36 us  [shards(): lax.all_to_all(jnp.stack([table] * lax.axis_size('x')), 'x', 0, 0)]
    all_to_all x1, starting transfers between devices: 3.41 us -> 10.3 us  [shards(): lax.all_to_all(table, 'lat', split_axis=0, concat_axis=1, tiled=True)]
    all_to_all x1, starting transfers between devices: 10.3 us -> 3.41 us  [shards(): lax.all_to_all(fourier, 'lat', split_axis=0, concat_axis=3, tiled=True)]
    all_to_all x0 -> x1, starting transfers between devices: none -> 4.29 us  [shards(): lax.all_to_all(jnp.stack([table] * lax.axis_size('x')), 'x', 0, 0)]
    all_to_all x1, starting transfers between devices: 4.8 us -> 8.3 us  [shards(): table = lax.all_to_all(table, 'g', split_axis=0, concat_axis=2, tiled=True)]
    all_to_all x1, starting transfers between devices: 8.3 us -> 4.8 us  [shards(): lax.all_to_all(fourier, 'g', split_axis=0, concat_axis=2, tiled=True)]
    another operation x0 -> x4, local copies, waits for them, and re-layouts: none -> 2.85 us
  transfers between devices with their start and end apart: 4 -> 5, of which waited for: 4 -> 5; matrix products, arithmetic and copies ran while one was open for 1% -> 3% of each run, Pallas kernels for 0% -> 0%
where the time goes in v1:
time: 110 us; the launch traced here: 109 us
  waiting for transfers between devices  46.3 us (42%)
  starting transfers between devices  31.1 us (28%)
  blocking collectives  14.9 us (14%)
  local copies, waits for them, and re-layouts  11.9 us (11%)
  matrix products  4.38 us (4%)
    all_to_all x1, blocking collectives, shards(): lax.all_to_all(block.astype(jnp.bfloat16), ('x', 'g'), split_axis=3, conc...  14.9 us
    all_to_all x1, waiting for transfers between devices, shards(): lax.all_to_all(fourier, 'lat', split_axis=0, concat_axis=3, tiled=True)  10.9 us
    all_to_all x1, starting transfers between devices, shards(): lax.all_to_all(table, 'lat', split_axis=0, concat_axis=1, tiled=True)  10.3 us
    all_to_all x1, waiting for transfers between devices, shards(): lax.all_to_all(table, 'lat', split_axis=0, concat_axis=1, tiled=True)  9.77 us
    all_to_all x1, waiting for transfers between devices, shards(): lax.all_to_all(jnp.stack([table] * lax.axis_size('x')), 'x', 0, 0)  9.36 us
    all_to_all x1, waiting for transfers between devices, shards(): lax.all_to_all(fourier, 'g', split_axis=0, concat_axis=2, tiled=True)  8.64 us
    all_to_all x1, starting transfers between devices, shards(): table = lax.all_to_all(table, 'g', split_axis=0, concat_axis=2, tiled=True)  8.3 us
    all_to_all x1, waiting for transfers between devices, shards(): table = lax.all_to_all(table, 'g', split_axis=0, concat_axis=2, tiled=True)  7.55 us
  transfers between devices with their start and end apart: 5, of which 5 were waited for; matrix products, arithmetic and copies ran while one was open for 3% of the time, Pallas kernels for 0%

profile of v1, /device:TPU:8, one launch (start us, length us, event | category | flops | bytes accessed | tf_op | source)
XLA Modules:
  0.0 108.9 jit_solution(15545663367335353828)
XLA Ops:
  0.0 2.0 %copy.20 = bf16[128,96,8]{1,2,0:T(8,128)(2,1)} copy(bf16[128,96,8]{0,2,1:T(8,128)(2,1)} %param.6) | data formatting | bytes 393216 | tf_op args[1]
  2.0 10.3 %all-to-all-start.2 = ((bf16[128,96,8]{1,2,0:T(8,128)(2,1)}), bf16[128,96,8]{1,2,0:T(8,128)(2,1)S(1)}, u32[]{:S(2)}, u32[]{:S(2)}) async-start(bf16[128,96,8]{1,2,0:T(8,128)(2,1)} %copy.20), calls=%async_computation.2 | async-start | bytes 524288 | tf_op jit(solution)/shard_map/all_to_all | solution.py:23
  12.3 2.1 %convolution_convert_fusion = bf16[256,384]{1,0:T(8,128)(2,1)S(1)} fusion(bf16[256,1536]{1,0:T(8,128)(2,1)} %constant.9, bf16[384,1536]{1,0:T(8,128)(2,1)} %bitcast.50), kind=kOutput, calls=%fused_computation.2 | convolution fusion | flops 302088192 | bytes 2162688 | tf_op jit(solution)/shard_map/dot_general | solution.py:29
  14.4 0.9 reshape.36
  15.3 9.8 %all-to-all-done.2 = bf16[128,96,8]{1,2,0:T(8,128)(2,1)S(1)} async-done(((bf16[128,96,8]{1,2,0:T(8,128)(2,1)}), bf16[128,96,8]{1,2,0:T(8,128)(2,1)S(1)}, u32[]{:S(2)}, u32[]{:S(2)}) %all-to-all-start.2) | async-done | bytes 196640 | tf_op jit(solution)/shard_map/all_to_all | solution.py:23
  25.1 3.4 %all-to-all-start = ((bf16[128,2,4,96]{3,2,1,0:T(4,128)(2,1)}), bf16[128,2,4,96]{3,2,1,0:T(4,128)(2,1)S(1)}, u32[]{:S(2)}, u32[]{:S(2)}) async-start(bf16[128,2,4,96]{3,2,1,0:T(4,128)(2,1)} %reshape.36), calls=%async_computation | async-start | bytes 524288 | tf_op jit(solution)/shard_map/all_to_all | solution.py:36
  28.5 0.2 copy.21
  28.7 0.9 all_to_all.68
  29.6 10.9 %all-to-all-done = bf16[128,2,4,96]{3,2,1,0:T(4,128)(2,1)S(1)} async-done(((bf16[128,2,4,96]{3,2,1,0:T(4,128)(2,1)}), bf16[128,2,4,96]{3,2,1,0:T(4,128)(2,1)S(1)}, u32[]{:S(2)}, u32[]{:S(2)}) %all-to-all-start) | async-done | bytes 196640 | tf_op jit(solution)/shard_map/all_to_all | solution.py:36
  40.5 8.3 %all-to-all-start.3 = ((bf16[16,768,8]{1,2,0:T(8,128)(2,1)}), bf16[16,768,8]{1,2,0:T(8,128)(2,1)S(1)}, u32[]{:S(2)}, u32[]{:S(2)}) async-start(bf16[16,768,8]{1,2,0:T(8,128)(2,1)} %all_to_all.68), calls=%async_computation.3 | async-start | bytes 393216 | tf_op jit(solution)/shard_map/all_to_all | solution.py:24
  48.8 0.3 copy.18
  49.2 0.9 all_to_all.61
  50.1 7.5 %all-to-all-done.3 = bf16[16,768,8]{1,2,0:T(8,128)(2,1)S(1)} async-done(((bf16[16,768,8]{1,2,0:T(8,128)(2,1)}), bf16[16,768,8]{1,2,0:T(8,128)(2,1)S(1)}, u32[]{:S(2)}, u32[]{:S(2)}) %all-to-all-start.3) | async-done | bytes 196640 | tf_op jit(solution)/shard_map/all_to_all | solution.py:24
  57.6 4.8 %all-to-all-start.1 = ((bf16[16,2,4,768]{3,2,1,0:T(4,128)(2,1)}), bf16[16,2,4,768]{3,2,1,0:T(4,128)(2,1)S(1)}, u32[]{:S(2)}, u32[]{:S(2)}) async-start(bf16[16,2,4,768]{3,2,1,0:T(4,128)(2,1)} %all_to_all.61), calls=%async_computation.1 | async-start | bytes 393216 | tf_op jit(solution)/shard_map/all_to_all | solution.py:37
  62.5 0.2 copy.22
  62.6 8.6 %all-to-all-done.1 = bf16[16,2,4,768]{3,2,1,0:T(4,128)(2,1)S(1)} async-done(((bf16[16,2,4,768]{3,2,1,0:T(4,128)(2,1)}), bf16[16,2,4,768]{3,2,1,0:T(4,128)(2,1)S(1)}, u32[]{:S(2)}, u32[]{:S(2)}) %all-to-all-start.1) | async-done | bytes 196640 | tf_op jit(solution)/shard_map/all_to_all | solution.py:37
  71.3 1.0 stack.10
  72.2 4.3 %all-to-all-start.4 = ((bf16[4,1,768,128]{3,2,1,0:T(8,128)(2,1)}), bf16[4,1,768,128]{3,2,1,0:T(8,128)(2,1)S(1)}, u32[]{:S(2)}, u32[]{:S(2)}) async-start(bf16[4,1,768,128]{3,2,1,0:T(8,128)(2,1)} %stack.10), calls=%async_computation.4 | async-start | bytes 1572864 | tf_op jit(solution)/shard_map/all_to_all | solution.py:26
  76.5 0.1 copy.19
  76.7 9.4 %all-to-all-done.4 = bf16[4,1,768,128]{3,2,1,0:T(8,128)(2,1)S(1)} async-done(((bf16[4,1,768,128]{3,2,1,0:T(8,128)(2,1)}), bf16[4,1,768,128]{3,2,1,0:T(8,128)(2,1)S(1)}, u32[]{:S(2)}, u32[]{:S(2)}) %all-to-all-start.4) | async-done | bytes 786464 | tf_op jit(solution)/shard_map/all_to_all | solution.py:26
  86.0 1.5 %copy.23 = bf16[1,768,4,128]{3,2,1,0:T(4,128)(2,1)} copy(bf16[1,768,4,128]{3,1,0,2:T(8,128)(2,1)S(1)} %bitcast.42) | data formatting | bytes 1572864 | tf_op jit(solution)/shard_map/reshape | solution.py:25
  87.5 1.6 %reshape.43 = bf16[768,512,1]{1,0,2:T(8,128)(2,1)S(1)} reshape(bf16[1,768,4,128]{3,2,1,0:T(4,128)(2,1)} %copy.23) | data formatting | bytes 1572864 | tf_op jit(solution)/shard_map/reshape.3
  89.2 0.3 fusion.2
  89.5 0.2 copy.24
  89.6 0.2 reshape.46
  89.8 14.9 %all_to_all.80 = bf16[64,2,512]{2,1,0:T(2,128)(2,1)S(1)} all-to-all(bf16[64,2,512]{2,1,0:T(2,128)(2,1)S(1)} %reshape.46), channel_id=1, replica_groups=mesh['x'=4,'g'=16,'lat'=8] {'x','g'}, dimensions={0} | all-to-all | bytes 262144 | tf_op jit(solution)/shard_map/all_to_all | solution.py:40
  104.8 0.2 reshape.47
  105.0 0.3 copy.26
  105.4 0.4 mul.23
  105.8 0.1 add.3
  106.0 2.0 %fusion = f32[8,16,2,256]{3,1,2,0:T(8,128)S(1)} fusion(f32[8,256,256]{2,1,0:T(8,128)S(1)} %copy-done, f32[8,16,2,256]{3,2,1,0:T(2,128)S(1)} %add.3), kind=kOutput, calls=%fused_computation | convolution fusion | flops 201326592 | bytes 2621440 | tf_op jit(solution)/shard_map/lij,lmcj->lmci/dot_general | solution.py:46
  108.0 0.9 copy.28
  (6 shorter events, 0.1 us)
Async XLA Ops:
  0.0 106.0 %copy-start = (f32[8,256,256]{2,1,0:T(8,128)S(1)}, f32[8,256,256]{2,1,0:T(8,128)}, u32[]{:S(2)}) copy-start(f32[8,256,256]{2,1,0:T(8,128)} %param.8) | copy-start | bytes 6291460
  2.0 23.1 %all-to-all-start.2 = ((bf16[128,96,8]{1,2,0:T(8,128)(2,1)}), bf16[128,96,8]{1,2,0:T(8,128)(2,1)S(1)}, u32[]{:S(2)}, u32[]{:S(2)}) async-start(bf16[128,96,8]{1,2,0:T(8,128)(2,1)} %copy.20), calls=%async_computation.2 | async-start | bytes 524288 | tf_op jit(solution)/shard_map/all_to_all | solution.py:23
  25.1 15.4 %all-to-all-start = ((bf16[128,2,4,96]{3,2,1,0:T(4,128)(2,1)}), bf16[128,2,4,96]{3,2,1,0:T(4,128)(2,1)S(1)}, u32[]{:S(2)}, u32[]{:S(2)}) async-start(bf16[128,2,4,96]{3,2,1,0:T(4,128)(2,1)} %reshape.36), calls=%async_computation | async-start | bytes 524288 | tf_op jit(solution)/shard_map/all_to_all | solution.py:36
  40.5 17.1 %all-to-all-start.3 = ((bf16[16,768,8]{1,2,0:T(8,128)(2,1)}), bf16[16,768,8]{1,2,0:T(8,128)(2,1)S(1)}, u32[]{:S(2)}, u32[]{:S(2)}) async-start(bf16[16,768,8]{1,2,0:T(8,128)(2,1)} %all_to_all.68), calls=%async_computation.3 | async-start | bytes 393216 | tf_op jit(solution)/shard_map/all_to_all | solution.py:24
  57.6 13.6 %all-to-all-start.1 = ((bf16[16,2,4,768]{3,2,1,0:T(4,128)(2,1)}), bf16[16,2,4,768]{3,2,1,0:T(4,128)(2,1)S(1)}, u32[]{:S(2)}, u32[]{:S(2)}) async-start(bf16[16,2,4,768]{3,2,1,0:T(4,128)(2,1)} %all_to_all.61), calls=%async_computation.1 | async-start | bytes 393216 | tf_op jit(solution)/shard_map/all_to_all | solution.py:37
  72.2 13.8 %all-to-all-start.4 = ((bf16[4,1,768,128]{3,2,1,0:T(8,128)(2,1)}), bf16[4,1,768,128]{3,2,1,0:T(8,128)(2,1)S(1)}, u32[]{:S(2)}, u32[]{:S(2)}) async-start(bf16[4,1,768,128]{3,2,1,0:T(8,128)(2,1)} %stack.10), calls=%async_computation.4 | async-start | bytes 1572864 | tf_op jit(solution)/shard_map/all_to_all | solution.py:26
  89.5 16.3 %copy-start.1 = (f32[8,16,2,256]{3,2,1,0:T(2,128)S(1)}, f32[8,16,2,256]{3,2,1,0:T(2,128)}, u32[]{:S(2)}) copy-start(f32[8,16,2,256]{3,2,1,0:T(2,128)} %param.7) | copy-start | bytes 786436
